TPU v7x, 512 devices: a whole 4x8x8 slice. The times are simulated.
512 devices in a mesh: freq: 16 (over z_lo, x), layer: 32 (over z_hi, y, core).
Axes of the slice: x: 4, y: 8, z: 8 (z_hi: 2, z_lo: 4; z = z_hi * 4 + z_lo), core: 2. Of those that a mesh axis runs over, the one named last changes fastest.
Arguments:
- conductivity: float32 [32, 128, 128], P('layer'), may hold values from 0.1 to 1
- background: float32 [16, 2, 2, 32, 128, 128], P('freq', None, None, 'layer'), may hold values from -6 to 6
- green: float32 [16, 2, 32, 256, 256], P('freq', None, None, 'layer'), may hold values from -2 to 2
- pair_table: int32 [32, 32], replicated, may hold values from 0 to 31, as said below
- stations: int32 [32, 128], P('layer'), may hold values from 0 to 16383, as said below
- observed: float32 [16, 2, 2, 32, 128], P('freq', None, None, 'layer'), may hold values from -6 to 6
- data_error: float32 [16, 2, 32, 128], P('freq', None, 'layer'), may hold values from 0.3 to 3
Outputs:
- gradient: float32 [32, 128, 128], P('layer')
Inputs may be any that keep to these rules, and one draw needn't show every extreme that they name: pair_table[i, j] == pair_table[j, i]. row-major cell index x * 128 + y within the station's layer; stations may share a cell.
All inputs are finite; a program needn't handle non-finite values.
Results may differ from a plain program's by a relative error of at most 0.000073.
Values sent between devices are 32-bit elements; how exact they have to be, the bound alone decides.
No kernel may reach another device: no remote copies, remote signals or barrier semaphores. Data moves between devices by JAX's collectives and lax.ppermute only.
A program may use at most 64 MiB of HBM per device.

v0:
```python
import math
import jax
import jax.numpy as jnp
from jax import lax
from jax.sharding import PartitionSpec as P

HIGHEST = lax.Precision.HIGHEST


def dft_tables(wave_count, cell_count):
    wave_ids = jnp.arange(wave_count, dtype=jnp.int32)[:, None]
    cell_ids = jnp.arange(cell_count, dtype=jnp.int32)[None, :]
    phases = wave_ids * cell_ids % wave_count
    angles = phases.astype(jnp.float32) * (2.0 * math.pi / wave_count)
    return (jnp.cos(angles), jnp.sin(angles))


def forward_rows(re_part, im_part, cosine_table, sine_table):
    cos_re = jnp.einsum("kx,...xy->...ky", cosine_table, re_part, precision=HIGHEST)
    cos_im = jnp.einsum("kx,...xy->...ky", cosine_table, im_part, precision=HIGHEST)
    sin_re = jnp.einsum("kx,...xy->...ky", sine_table, re_part, precision=HIGHEST)
    sin_im = jnp.einsum("kx,...xy->...ky", sine_table, im_part, precision=HIGHEST)
    return (cos_re + sin_im, cos_im - sin_re)


def forward_cols(re_part, im_part, cosine_table, sine_table):
    cos_re = jnp.einsum("...y,ky->...k", re_part, cosine_table, precision=HIGHEST)
    cos_im = jnp.einsum("...y,ky->...k", im_part, cosine_table, precision=HIGHEST)
    sin_re = jnp.einsum("...y,ky->...k", re_part, sine_table, precision=HIGHEST)
    sin_im = jnp.einsum("...y,ky->...k", im_part, sine_table, precision=HIGHEST)
    return (cos_re + sin_im, cos_im - sin_re)


def inverse_cols(re_part, im_part, cosine_table, sine_table):
    scale = 1.0 / cosine_table.shape[0]
    cos_re = jnp.einsum("...k,ky->...y", re_part, cosine_table, precision=HIGHEST)
    cos_im = jnp.einsum("...k,ky->...y", im_part, cosine_table, precision=HIGHEST)
    sin_re = jnp.einsum("...k,ky->...y", re_part, sine_table, precision=HIGHEST)
    sin_im = jnp.einsum("...k,ky->...y", im_part, sine_table, precision=HIGHEST)
    return ((cos_re - sin_im) * scale, (cos_im + sin_re) * scale)


def inverse_rows(re_part, im_part, cosine_table, sine_table):
    scale = 1.0 / cosine_table.shape[0]
    cos_re = jnp.einsum("kx,...ky->...xy", cosine_table, re_part, precision=HIGHEST)
    cos_im = jnp.einsum("kx,...ky->...xy", cosine_table, im_part, precision=HIGHEST)
    sin_re = jnp.einsum("kx,...ky->...xy", sine_table, re_part, precision=HIGHEST)
    sin_im = jnp.einsum("kx,...ky->...xy", sine_table, im_part, precision=HIGHEST)
    return ((cos_re - sin_im) * scale, (cos_im + sin_re) * scale)


def mix_layers(spec_real, spec_imag, green_real, green_imag, pair_table):

    def one_receiver(table_row):
        row_real = jnp.take(green_real, table_row, axis=0)
        row_imag = jnp.take(green_imag, table_row, axis=0)
        out_real = jnp.sum(row_real * spec_real - row_imag * spec_imag, axis=1)
        out_imag = jnp.sum(row_real * spec_imag + row_imag * spec_real, axis=1)
        return (out_real, out_imag)

    mixed_real, mixed_imag = lax.map(one_receiver, pair_table)
    return (jnp.moveaxis(mixed_real, 0, 1), jnp.moveaxis(mixed_imag, 0, 1))


def apply_green(src_real, src_imag, green_real, green_imag, pair_table):
    x_cells = src_real.shape[-2]
    y_cells = src_real.shape[-1]
    cosine_x, sine_x = dft_tables(2 * x_cells, x_cells)
    cosine_y, sine_y = dft_tables(2 * y_cells, y_cells)
    rows_real, rows_imag = forward_rows(src_real, src_imag, cosine_x, sine_x)
    spec_real, spec_imag = forward_cols(rows_real, rows_imag, cosine_y, sine_y)
    mixed = mix_layers(
        lax.all_to_all(spec_real, "layer", split_axis=2, concat_axis=1, tiled=True),
        lax.all_to_all(spec_imag, "layer", split_axis=2, concat_axis=1, tiled=True),
        green_real,
        green_imag,
        pair_table,
    )
    back_real, back_imag = (
        lax.all_to_all(mixed[0], "layer", split_axis=1, concat_axis=2, tiled=True),
        lax.all_to_all(mixed[1], "layer", split_axis=1, concat_axis=2, tiled=True),
    )
    cols_real, cols_imag = inverse_cols(back_real, back_imag, cosine_y, sine_y)
    return inverse_rows(cols_real, cols_imag, cosine_x, sine_x)


def station_values(total_real, total_imag, stations, measured, errors):
    pol_count = total_real.shape[0]
    layer_count = total_real.shape[1]
    flat_real = total_real.reshape(pol_count, layer_count, -1)
    flat_imag = total_imag.reshape(pol_count, layer_count, -1)
    station_idx = jnp.broadcast_to(stations[None], (pol_count,) + stations.shape)
    pred_real = jnp.take_along_axis(flat_real, station_idx, axis=2)
    pred_imag = jnp.take_along_axis(flat_imag, station_idx, axis=2)
    weight = errors * errors
    return ((pred_real - measured[:, 0]) / weight, (pred_imag - measured[:, 1]) / weight)


def scatter_source(resid_real, resid_imag, stations, field_shape):
    pol_count, layer_count = (field_shape[0], field_shape[1])
    cells = field_shape[2] * field_shape[3]
    layer_ids = jnp.arange(layer_count, dtype=jnp.int32)[:, None]
    source_real = (
        jnp.zeros((pol_count, layer_count, cells), jnp.float32)
        .at[:, layer_ids, stations]
        .add(resid_real)
    )
    source_imag = (
        jnp.zeros((pol_count, layer_count, cells), jnp.float32)
        .at[:, layer_ids, stations]
        .add(-resid_imag)
    )
    return (source_real.reshape(field_shape), source_imag.reshape(field_shape))


def per_device(conductivity, background, green, pair_table, stations, observed, data_error):
    field_pair = background[0]
    bg_real = field_pair[:, 0]
    bg_imag = field_pair[:, 1]
    green_real = green[0, 0]
    green_imag = green[0, 1]
    scat_real, scat_imag = apply_green(
        conductivity * bg_real, conductivity * bg_imag, green_real, green_imag, pair_table
    )
    total_real = bg_real + scat_real
    total_imag = bg_imag + scat_imag
    resid_real, resid_imag = station_values(
        total_real, total_imag, stations, observed[0], data_error[0]
    )
    source_real, source_imag = scatter_source(resid_real, resid_imag, stations, total_real.shape)
    adj_real, adj_imag = apply_green(source_real, source_imag, green_real, green_imag, pair_table)
    local_term = jnp.sum(total_real * adj_real - total_imag * adj_imag, axis=0)
    return lax.psum(local_term, "freq")


def solution(mesh):
    in_specs = (
        P("layer", None, None),
        P("freq", None, None, "layer", None, None),
        P("freq", None, None, "layer", None),
        P(),
        P("layer", None),
        P("freq", None, None, "layer", None),
        P("freq", None, "layer", None),
    )
    out_specs = P("layer", None, None)
    return jax.shard_map(
        per_device, mesh=mesh, in_specs=in_specs, out_specs=out_specs, check_vma=False
    )
```

profile of v0, /device:TPU:8, one launch (start us, length us, event | category | flops | bytes accessed | tf_op | source)
XLA Modules:
  0.0 622.1 jit_solution(12864283717387447946)
XLA Ops:
  6.5 1.1 copy.68
  7.7 0.9 copy.69
  8.6 0.9 fusion.97
  10.4 0.9 fusion.13
  11.2 1.1 fusion.95
  12.3 0.9 fusion.12
  13.2 1.1 fusion.9
  14.2 1.2 copy.72
  15.4 16.1 %all-to-all-start = ((f32[2,1,256,256]{3,0,1,2:T(2,128)}), f32[2,1,256,256]{3,0,1,2:T(2,128)S(1)}, u32[]{:S(2)}, u32[]{:S(2)}) async-start(f32[2,1,256,256]{3,0,1,2:T(2,128)} %copy.72), calls=%async_computation | async-start | bytes 1048576 | tf_op jit(solution)/shard_map/all_to_all | solution.py:73
  31.6 1.1 fusion.91
  32.7 1.1 fusion.8
  33.7 1.2 copy.75
  34.9 18.5 %all-to-all-done = f32[2,1,256,256]{3,0,1,2:T(2,128)S(1)} async-done(((f32[2,1,256,256]{3,0,1,2:T(2,128)}), f32[2,1,256,256]{3,0,1,2:T(2,128)S(1)}, u32[]{:S(2)}, u32[]{:S(2)}) %all-to-all-start) | async-done | bytes 524320 | tf_op jit(solution)/shard_map/all_to_all | solution.py:73
  53.4 4.3 all-to-all-start.1
  57.8 21.8 %all-to-all-done.1 = f32[2,1,256,256]{3,0,1,2:T(2,128)S(1)} async-done(((f32[2,1,256,256]{3,0,1,2:T(2,128)}), f32[2,1,256,256]{3,0,1,2:T(2,128)S(1)}, u32[]{:S(2)}, u32[]{:S(2)}) %all-to-all-start.1) | async-done | bytes 524320 | tf_op jit(solution)/shard_map/all_to_all | solution.py:74
  79.7 0.9 broadcast.77.clone
  81.4 88.7 %while.24 = (s32[]{:T(128)}, f32[32,2,8,256]{3,2,1,0:T(8,128)}, f32[32,2,8,256]{3,2,1,0:T(8,128)}, s32[32,32]{1,0:T(8,128)}, f32[32,8,256]{2,1,0:T(8,128)S(1)}, ...) while((s32[]{:T(128)}, f32[32,2,8,256]{3,2,1,0:T(8,128)}, ...), condition=%wide.region_3.5_spmd, body=%wide.region_0.4_spmd.sunk | while | flops 1172674 | bytes 3773729 | solution.py:61
  170.2 4.3 all-to-all-start.2
  174.6 21.9 %all-to-all-done.2 = f32[2,32,8,256]{3,2,0,1:T(8,128)S(1)} async-done(((f32[2,32,8,256]{3,2,0,1:T(8,128)}), f32[2,32,8,256]{3,2,0,1:T(8,128)S(1)}, u32[]{:S(2)}, u32[]{:S(2)}) %all-to-all-start.2) | async-done | bytes 524320 | tf_op jit(solution)/shard_map/all_to_all | solution.py:80
  196.4 4.9 all-to-all-start.3
  201.4 1.1 fusion.42
  202.5 20.7 %all-to-all-done.3 = f32[2,32,8,256]{3,2,0,1:T(8,128)S(1)} async-done(((f32[2,32,8,256]{3,2,0,1:T(8,128)}), f32[2,32,8,256]{3,2,0,1:T(8,128)S(1)}, u32[]{:S(2)}, u32[]{:S(2)}) %all-to-all-start.3) | async-done | bytes 524320 | tf_op jit(solution)/shard_map/all_to_all | solution.py:81
  223.1 1.1 fusion.14
  224.2 1.0 fusion.88
  225.2 1.1 fusion.38
  226.2 1.1 fusion.15
  227.3 1.0 fusion.83
  228.3 1.0 fusion.26
  229.5 1.0 fusion.27
  230.7 2.5 gather_fusion.4
  233.2 2.5 gather_fusion.5
  235.8 4.9 scatter_custom_fusion.1
  240.7 6.6 %copy.90 = f32[2,128,128]{1,2,0:T(8,128)S(1)} copy(f32[2,128,128]{0,2,1:T(8,128)} %bitcast.285) | data formatting | bytes 262144 | tf_op jit(solution)/shard_map/reshape.56
  247.2 0.9 fusion.79
  248.2 4.7 scatter_custom_fusion
  253.0 6.6 %copy.85 = f32[2,128,128]{1,2,0:T(8,128)S(1)} copy(f32[2,128,128]{0,2,1:T(8,128)} %bitcast.284) | data formatting | bytes 262144 | tf_op jit(solution)/shard_map/reshape.49
  259.5 0.9 fusion.85
  260.4 0.9 fusion.10
  261.3 1.1 fusion.77
  262.3 0.9 fusion.11
  263.2 1.1 fusion.6
  264.3 1.2 copy.98
  265.5 4.7 all-to-all-start.5
  270.1 1.1 fusion.81
  271.2 1.1 fusion.7
  272.3 1.2 copy.95
  273.5 18.5 %all-to-all-done.5 = f32[2,1,256,256]{3,0,1,2:T(2,128)S(1)} async-done(((f32[2,1,256,256]{3,0,1,2:T(2,128)}), f32[2,1,256,256]{3,0,1,2:T(2,128)S(1)}, u32[]{:S(2)}, u32[]{:S(2)}) %all-to-all-start.5) | async-done | bytes 524320 | tf_op jit(solution)/shard_map/all_to_all | solution.py:74
  292.0 4.3 all-to-all-start.4
  296.4 21.9 %all-to-all-done.4 = f32[2,1,256,256]{3,0,1,2:T(2,128)S(1)} async-done(((f32[2,1,256,256]{3,0,1,2:T(2,128)}), f32[2,1,256,256]{3,0,1,2:T(2,128)S(1)}, u32[]{:S(2)}, u32[]{:S(2)}) %all-to-all-start.4) | async-done | bytes 524320 | tf_op jit(solution)/shard_map/all_to_all | solution.py:73
  318.3 0.9 broadcast.77
  319.2 88.3 %while.25 = (s32[]{:T(128)}, f32[32,2,8,256]{3,2,1,0:T(8,128)}, f32[32,2,8,256]{3,2,1,0:T(8,128)S(1)}, s32[32,32]{1,0:T(8,128)}, f32[32,8,256]{2,1,0:T(8,128)S(1...) while((s32[]{:T(128)}, f32[32,2,8,256]{3,2,1,0:T(8,128)}, ...), condition=%wide.region_9.12_spmd, body=%wide.region_6.11_spmd.sunk | while | flops 1172674 | bytes 3773729 | solution.py:61
  407.5 25.4 %all_to_all.84 = f32[2,32,8,256]{3,2,0,1:T(8,128)S(1)} all-to-all(f32[2,32,8,256]{3,2,0,1:T(8,128)S(1)} %bitcast.292), channel_id=1, replica_groups=mesh['freq'=16,'layer'=32] {'layer'}, dimensions={1} | all-to-all | bytes 1048576 | tf_op jit(solution)/shard_map/all_to_all | solution.py:81
  432.9 4.3 all-to-all-start.6
  437.2 1.1 fusion.32
  438.3 20.8 %all-to-all-done.6 = f32[2,32,8,256]{3,2,0,1:T(8,128)S(1)} async-done(((f32[2,32,8,256]{3,2,0,1:T(8,128)}), f32[2,32,8,256]{3,2,0,1:T(8,128)S(1)}, u32[]{:S(2)}, u32[]{:S(2)}) %all-to-all-start.6) | async-done | bytes 524320 | tf_op jit(solution)/shard_map/all_to_all | solution.py:80
  459.1 1.1 fusion.17
  460.2 1.0 fusion.71
  461.2 1.1 fusion.36
  462.3 1.1 fusion.16
  463.3 1.0 fusion.74
  464.3 1.0 fusion.30
  465.3 1.6 fusion.31
  466.9 146.6 %all-reduce.3.cloned.1.call-done = f32[1,128,128]{1,2,0:T(8,128)} async-done(((f32[1,128,128]{1,2,0:T(8,128)}), f32[1,128,128]{1,2,0:T(8,128)}) %all-reduce.3.cloned.1.call-update) | async-done | bytes 65552 | tf_op jit(solution)/shard_map/psum | solution.py:133
  613.5 1.6 copy.107
  (481 shorter events, 177.5 us)
Async XLA Ops:
  6.5 51.2 %copy-start = (f32[1,2,32,8,256]{4,3,2,1,0:T(8,128)S(1)}, f32[1,2,32,8,256]{4,3,2,1,0:T(8,128)}, u32[]{:S(2)}) copy-start(f32[1,2,32,8,256]{4,3,2,1,0:T(8,128)} %param.17) | copy-start | bytes 1572868
  15.4 38.0 %all-to-all-start = ((f32[2,1,256,256]{3,0,1,2:T(2,128)}), f32[2,1,256,256]{3,0,1,2:T(2,128)S(1)}, u32[]{:S(2)}, u32[]{:S(2)}) async-start(f32[2,1,256,256]{3,0,1,2:T(2,128)} %copy.72), calls=%async_computation | async-start | bytes 1048576 | tf_op jit(solution)/shard_map/all_to_all | solution.py:73
  53.4 26.3 %all-to-all-start.1 = ((f32[2,1,256,256]{3,0,1,2:T(2,128)}), f32[2,1,256,256]{3,0,1,2:T(2,128)S(1)}, u32[]{:S(2)}, u32[]{:S(2)}) async-start(f32[2,1,256,256]{3,0,1,2:T(2,128)} %copy.75), calls=%async_computation.1 | async-start | bytes 1048576 | tf_op jit(solution)/shard_map/all_to_all | solution.py:74
  81.4 93.1 %copy-start.3 = (f32[1,2,2,1,128]{4,3,2,1,0:T(1,128)S(1)}, f32[1,2,2,1,128]{4,3,2,1,0:T(1,128)}, u32[]{:S(2)}) copy-start(f32[1,2,2,1,128]{4,3,2,1,0:T(1,128)} %param.20) | copy-start | bytes 6148
  81.4 93.1 %copy-start.1 = (f32[1,2,1,128]{3,2,1,0:T(1,128)S(1)}, f32[1,2,1,128]{3,2,1,0:T(1,128)}, u32[]{:S(2)}) copy-start(f32[1,2,1,128]{3,2,1,0:T(1,128)} %param.21) | copy-start | bytes 3076
  81.4 93.1 %copy-start.2 = (s32[1,128]{1,0:T(1,128)S(1)}, s32[1,128]{1,0:T(1,128)}, u32[]{:S(2)}) copy-start(s32[1,128]{1,0:T(1,128)} %param.19) | copy-start | bytes 1540
  170.2 26.3 %all-to-all-start.2 = ((f32[2,32,8,256]{3,2,0,1:T(8,128)}), f32[2,32,8,256]{3,2,0,1:T(8,128)S(1)}, u32[]{:S(2)}, u32[]{:S(2)}) async-start(f32[2,32,8,256]{3,2,0,1:T(8,128)} %bitcast.29), calls=%async_computation.2 | async-start | bytes 1048576 | tf_op jit(solution)/shard_map/all_to_all | solution.py:80
  196.4 26.7 %all-to-all-start.3 = ((f32[2,32,8,256]{3,2,0,1:T(8,128)}), f32[2,32,8,256]{3,2,0,1:T(8,128)S(1)}, u32[]{:S(2)}, u32[]{:S(2)}) async-start(f32[2,32,8,256]{3,2,0,1:T(8,128)} %bitcast.31), calls=%async_computation.3 | async-start | bytes 1048576 | tf_op jit(solution)/shard_map/all_to_all | solution.py:81
  265.5 26.5 %all-to-all-start.5 = ((f32[2,1,256,256]{3,0,1,2:T(2,128)}), f32[2,1,256,256]{3,0,1,2:T(2,128)S(1)}, u32[]{:S(2)}, u32[]{:S(2)}) async-start(f32[2,1,256,256]{3,0,1,2:T(2,128)} %copy.98), calls=%async_computation.5 | async-start | bytes 1048576 | tf_op jit(solution)/shard_map/all_to_all | solution.py:74
  292.0 26.3 %all-to-all-start.4 = ((f32[2,1,256,256]{3,0,1,2:T(2,128)}), f32[2,1,256,256]{3,0,1,2:T(2,128)S(1)}, u32[]{:S(2)}, u32[]{:S(2)}) async-start(f32[2,1,256,256]{3,0,1,2:T(2,128)} %copy.95), calls=%async_computation.4 | async-start | bytes 1048576 | tf_op jit(solution)/shard_map/all_to_all | solution.py:73
  432.9 26.3 %all-to-all-start.6 = ((f32[2,32,8,256]{3,2,0,1:T(8,128)}), f32[2,32,8,256]{3,2,0,1:T(8,128)S(1)}, u32[]{:S(2)}, u32[]{:S(2)}) async-start(f32[2,32,8,256]{3,2,0,1:T(8,128)} %bitcast.74), calls=%async_computation.6 | async-start | bytes 1048576 | tf_op jit(solution)/shard_map/all_to_all | solution.py:80
  437.2 176.3 %all-reduce.3.cloned.1.call-start = ((), (), s32[]{:S(2)}) async-start(), calls=%async_computation.8 | async-start | bytes 131072 | tf_op jit(solution)/shard_map/psum | solution.py:133
Sparse Core Ops, SparseCore 0:
  467.0 146.4 all-reduce.2
where the time goes:
time: 633 us; the launch traced here: 622 us
  waiting for transfers between devices  291 us (46%)
  local copies, waits for them, and re-layouts  144 us (23%)
  other arithmetic  70.2 us (11%)
  starting transfers between devices  43 us (7%)
  matrix products  32.3 us (5%)
  blocking collectives  25.4 us (4%)
  between operations  14.1 us (2%)
    psum x1, waiting for transfers between devices, per_device(): return lax.psum(local_term, 'freq')  147 us
    and x64, other arithmetic, one_receiver(): row_real = jnp.take(green_real, table_row, axis=0)  44.6 us
    all_to_all x2, waiting for transfers between devices, apply_green(): lax.all_to_all(mixed[0], 'layer', split_axis=1, concat_axis=2, tiled=True)  42.7 us
    all_to_all x2, waiting for transfers between devices, apply_green(): lax.all_to_all(spec_real, 'layer', split_axis=2, concat_axis=1, tiled=True)  40.4 us
    all_to_all x2, waiting for transfers between devices, apply_green(): lax.all_to_all(spec_imag, 'layer', split_axis=2, concat_axis=1, tiled=True)  40.3 us
    dynamic_update_slice x64, local copies, waits for them, and re-layouts, mix_layers(): mixed_real, mixed_imag = lax.map(one_receiver, pair_table)  39.3 us
    gather x64, local copies, waits for them, and re-layouts, one_receiver(): row_real = jnp.take(green_real, table_row, axis=0)  37.5 us
    gather x64, local copies, waits for them, and re-layouts, one_receiver(): row_imag = jnp.take(green_imag, table_row, axis=0)  37.5 us
  transfers between devices with their start and end apart: 8, of which 8 were waited for; matrix products, arithmetic and copies ran while one was open for 1% of the time, Pallas kernels for 0%

commit v1 on v0

--- a/solution.py
+++ b/solution.py
@@ -77,7 +77,12 @@
         pair_table,
     )
     back_real, back_imag = (
-        lax.all_to_all(mixed[0], "layer", split_axis=1, concat_axis=2, tiled=True),
+        jnp.concatenate(
+            lax.all_to_all(
+                jnp.stack(jnp.split(mixed[0], lax.axis_size("layer"), axis=1)), "layer", 0, 0
+            ),
+            axis=2,
+        ),
         lax.all_to_all(mixed[1], "layer", split_axis=1, concat_axis=2, tiled=True),
     )
     cols_real, cols_imag = inverse_cols(back_real, back_imag, cosine_y, sine_y)

time: 633 us -> 669 us (1.057)
  local copies, waits for them, and re-layouts: 144 us -> 181 us
  blocking collectives: 25.4 us -> 0 us
  waiting for transfers between devices: 291 us -> 310 us
    unnamed x12 -> x74, local copies, waits for them, and re-layouts: 1.36 us -> 38.6 us
    all_to_all x1 -> x0, blocking collectives: 25.4 us -> none  [apply_green(): lax.all_to_all(mixed[1], 'layer', split_axis=1, concat_axis=2, tiled=True)]
    all_to_all x1 -> x2, waiting for transfers between devices: 20.7 us -> 39.6 us  [apply_green(): lax.all_to_all(mixed[1], 'layer', split_axis=1, concat_axis=2, tiled=True)]
    another operation x6 -> x8, local copies, waits for them, and re-layouts: 15.7 us -> 16.2 us
  transfers between devices with their start and end apart: 8 -> 9, of which waited for: 8 -> 9; matrix products, arithmetic and copies ran while one was open for 1% -> 2% of each run, Pallas kernels for 0% -> 0%
where the time goes in v1:
time: 669 us; the launch traced here: 657 us
  waiting for transfers between devices  310 us (46%)
  local copies, waits for them, and re-layouts  181 us (27%)
  other arithmetic  70.2 us (10%)
  starting transfers between devices  47.1 us (7%)
  matrix products  32.3 us (5%)
  between operations  14.4 us (2%)
    psum x1, waiting for transfers between devices, per_device(): return lax.psum(local_term, 'freq')  147 us
    and x64, other arithmetic, one_receiver(): row_real = jnp.take(green_real, table_row, axis=0)  44.6 us
    all_to_all x2, waiting for transfers between devices, apply_green(): lax.all_to_all(jnp.stack(jnp.split(mixed[0], lax.axis_size('layer'), axis...  42.7 us
    all_to_all x2, waiting for transfers between devices, apply_green(): lax.all_to_all(spec_real, 'layer', split_axis=2, concat_axis=1, tiled=True)  40.4 us
    all_to_all x2, waiting for transfers between devices, apply_green(): lax.all_to_all(spec_imag, 'layer', split_axis=2, concat_axis=1, tiled=True)  40.3 us
    all_to_all x2, waiting for transfers between devices, apply_green(): lax.all_to_all(mixed[1], 'layer', split_axis=1, concat_axis=2, tiled=True)  39.6 us
    dynamic_update_slice x64, local copies, waits for them, and re-layouts, mix_layers(): mixed_real, mixed_imag = lax.map(one_receiver, pair_table)  38.8 us
    unnamed x74, local copies, waits for them, and re-layouts  38.6 us
  transfers between devices with their start and end apart: 9, of which 9 were waited for; matrix products, arithmetic and copies ran while one was open for 2% of the time, Pallas kernels for 0%

profile of v1, /device:TPU:8, one launch (start us, length us, event | category | flops | bytes accessed | tf_op | source)
XLA Modules:
  0.0 657.2 jit_solution(10048150889593668214)
XLA Ops:
  6.5 1.1 copy.68
  7.7 0.9 copy.69
  8.6 0.9 fusion.97
  9.5 0.9 fusion.93
  10.4 0.9 fusion.13
  11.2 1.1 fusion.95
  12.3 0.9 fusion.12
  13.2 1.1 fusion.9
  14.2 1.2 copy.72
  15.4 16.1 %all-to-all-start = ((f32[2,1,256,256]{3,0,1,2:T(2,128)}), f32[2,1,256,256]{3,0,1,2:T(2,128)S(1)}, u32[]{:S(2)}, u32[]{:S(2)}) async-start(f32[2,1,256,256]{3,0,1,2:T(2,128)} %copy.72), calls=%async_computation | async-start | bytes 1048576 | tf_op jit(solution)/shard_map/all_to_all | solution.py:73
  31.6 1.1 fusion.91
  32.7 1.1 fusion.8
  33.7 1.2 copy.75
  34.9 18.5 %all-to-all-done = f32[2,1,256,256]{3,0,1,2:T(2,128)S(1)} async-done(((f32[2,1,256,256]{3,0,1,2:T(2,128)}), f32[2,1,256,256]{3,0,1,2:T(2,128)S(1)}, u32[]{:S(2)}, u32[]{:S(2)}) %all-to-all-start) | async-done | bytes 524320 | tf_op jit(solution)/shard_map/all_to_all | solution.py:73
  53.4 4.3 all-to-all-start.1
  57.8 21.8 %all-to-all-done.1 = f32[2,1,256,256]{3,0,1,2:T(2,128)S(1)} async-done(((f32[2,1,256,256]{3,0,1,2:T(2,128)}), f32[2,1,256,256]{3,0,1,2:T(2,128)S(1)}, u32[]{:S(2)}, u32[]{:S(2)}) %all-to-all-start.1) | async-done | bytes 524320 | tf_op jit(solution)/shard_map/all_to_all | solution.py:74
  80.6 88.3 %while.24 = (s32[]{:T(128)}, f32[32,2,8,256]{3,2,1,0:T(8,128)S(1)}, f32[32,2,8,256]{3,2,1,0:T(8,128)}, s32[32,32]{1,0:T(8,128)}, f32[32,8,256]{2,1,0:T(8,128)S(1...) while((s32[]{:T(128)}, f32[32,2,8,256]{3,2,1,0:T(8,128)S(1)}, ...), condition=%wide.region_3.5_spmd, body=%wide.region_0.4_spmd.sunk | while | flops 1172674 | bytes 3773729 | solution.py:61
  188.2 4.3 all-to-all-start.2
  192.6 21.9 %all-to-all-done.2 = f32[32,2,1,8,256]{4,3,1,2,0:T(8,128)S(1)} async-done(((f32[32,2,1,8,256]{4,3,1,2,0:T(8,128)}), f32[32,2,1,8,256]{4,3,1,2,0:T(8,128)S(1)}, u32[]{:S(2)}, u32[]{:S(2)}) %all-to-all-start.2) | async-done | bytes 524320 | tf_op jit(solution)/shard_map/all_to_all | solution.py:81
  214.4 4.6 all-to-all-start.3
  219.1 1.1 fusion.42
  220.2 20.7 %all-to-all-done.3 = f32[2,32,8,256]{3,2,0,1:T(8,128)S(1)} async-done(((f32[2,32,8,256]{3,2,0,1:T(8,128)}), f32[2,32,8,256]{3,2,0,1:T(8,128)S(1)}, u32[]{:S(2)}, u32[]{:S(2)}) %all-to-all-start.3) | async-done | bytes 524320 | tf_op jit(solution)/shard_map/all_to_all | solution.py:86
  240.9 1.1 fusion.14
  241.9 1.0 fusion.88
  242.9 1.1 fusion.38
  244.0 1.1 fusion.15
  245.1 1.0 fusion.83
  246.0 1.0 fusion.26
  247.2 1.0 fusion.27
  248.4 2.5 gather_fusion.4
  250.9 2.5 gather_fusion.5
  253.5 4.9 scatter_custom_fusion.1
  258.4 6.6 copy.90
  265.0 0.9 fusion.79
  266.0 4.7 scatter_custom_fusion
  270.7 6.6 copy.85
  277.3 0.9 fusion.85
  278.1 0.9 fusion.10
  279.0 1.1 fusion.77
  280.1 0.9 fusion.11
  281.0 1.1 fusion.6
  282.0 1.2 copy.98
  283.2 4.7 all-to-all-start.5
  287.9 1.1 fusion.81
  289.0 1.1 fusion.7
  290.1 1.2 copy.95
  291.3 18.5 %all-to-all-done.5 = f32[2,1,256,256]{3,0,1,2:T(2,128)S(1)} async-done(((f32[2,1,256,256]{3,0,1,2:T(2,128)}), f32[2,1,256,256]{3,0,1,2:T(2,128)S(1)}, u32[]{:S(2)}, u32[]{:S(2)}) %all-to-all-start.5) | async-done | bytes 524320 | tf_op jit(solution)/shard_map/all_to_all | solution.py:74
  309.7 4.3 all-to-all-start.4
  314.1 21.9 %all-to-all-done.4 = f32[2,1,256,256]{3,0,1,2:T(2,128)S(1)} async-done(((f32[2,1,256,256]{3,0,1,2:T(2,128)}), f32[2,1,256,256]{3,0,1,2:T(2,128)S(1)}, u32[]{:S(2)}, u32[]{:S(2)}) %all-to-all-start.4) | async-done | bytes 524320 | tf_op jit(solution)/shard_map/all_to_all | solution.py:73
  337.0 88.3 %while.25 = (s32[]{:T(128)}, f32[32,2,8,256]{3,2,1,0:T(8,128)S(1)}, f32[32,2,8,256]{3,2,1,0:T(8,128)}, s32[32,32]{1,0:T(8,128)}, f32[32,8,256]{2,1,0:T(8,128)S(1...) while((s32[]{:T(128)}, f32[32,2,8,256]{3,2,1,0:T(8,128)S(1)}, ...), condition=%wide.region_9.12_spmd, body=%wide.region_6.11_spmd.sunk | while | flops 1172674 | bytes 3773729 | solution.py:61
  441.5 4.3 all-to-all-start.7
  448.8 18.9 %all-to-all-done.7 = f32[2,32,8,256]{3,2,0,1:T(8,128)S(1)} async-done(((f32[2,32,8,256]{3,2,0,1:T(8,128)}), f32[2,32,8,256]{3,2,0,1:T(8,128)S(1)}, u32[]{:S(2)}, u32[]{:S(2)}) %all-to-all-start.7) | async-done | bytes 524320 | tf_op jit(solution)/shard_map/all_to_all | solution.py:86
  467.7 4.3 all-to-all-start.6
  472.1 1.1 fusion.32
  473.2 20.8 %all-to-all-done.6 = f32[32,2,1,8,256]{4,3,1,2,0:T(8,128)S(1)} async-done(((f32[32,2,1,8,256]{4,3,1,2,0:T(8,128)}), f32[32,2,1,8,256]{4,3,1,2,0:T(8,128)S(1)}, u32[]{:S(2)}, u32[]{:S(2)}) %all-to-all-start.6) | async-done | bytes 524320 | tf_op jit(solution)/shard_map/all_to_all | solution.py:81
  494.0 1.1 fusion.17
  495.1 1.0 fusion.71
  496.0 1.1 fusion.36
  497.1 1.1 fusion.16
  498.2 1.0 fusion.74
  499.2 1.0 fusion.30
  500.1 1.6 fusion.31
  501.8 146.6 %all-reduce.3.cloned.1.call-done = f32[1,128,128]{1,2,0:T(8,128)} async-done(((f32[1,128,128]{1,2,0:T(8,128)}), f32[1,128,128]{1,2,0:T(8,128)}) %all-reduce.3.cloned.1.call-update) | async-done | bytes 65552 | tf_op jit(solution)/shard_map/psum | solution.py:138
  648.4 1.6 copy.107
  (546 shorter events, 215.5 us)
Async XLA Ops:
  6.5 51.2 %copy-start = (f32[1,2,32,8,256]{4,3,2,1,0:T(8,128)S(1)}, f32[1,2,32,8,256]{4,3,2,1,0:T(8,128)}, u32[]{:S(2)}) copy-start(f32[1,2,32,8,256]{4,3,2,1,0:T(8,128)} %param.17) | copy-start | bytes 1572868
  15.4 38.0 %all-to-all-start = ((f32[2,1,256,256]{3,0,1,2:T(2,128)}), f32[2,1,256,256]{3,0,1,2:T(2,128)S(1)}, u32[]{:S(2)}, u32[]{:S(2)}) async-start(f32[2,1,256,256]{3,0,1,2:T(2,128)} %copy.72), calls=%async_computation | async-start | bytes 1048576 | tf_op jit(solution)/shard_map/all_to_all | solution.py:73
  53.4 26.3 %all-to-all-start.1 = ((f32[2,1,256,256]{3,0,1,2:T(2,128)}), f32[2,1,256,256]{3,0,1,2:T(2,128)S(1)}, u32[]{:S(2)}, u32[]{:S(2)}) async-start(f32[2,1,256,256]{3,0,1,2:T(2,128)} %copy.75), calls=%async_computation.1 | async-start | bytes 1048576 | tf_op jit(solution)/shard_map/all_to_all | solution.py:74
  80.6 111.9 %copy-start.3 = (f32[1,2,2,1,128]{4,3,2,1,0:T(1,128)S(1)}, f32[1,2,2,1,128]{4,3,2,1,0:T(1,128)}, u32[]{:S(2)}) copy-start(f32[1,2,2,1,128]{4,3,2,1,0:T(1,128)} %param.20) | copy-start | bytes 6148
  80.6 111.9 %copy-start.1 = (f32[1,2,1,128]{3,2,1,0:T(1,128)S(1)}, f32[1,2,1,128]{3,2,1,0:T(1,128)}, u32[]{:S(2)}) copy-start(f32[1,2,1,128]{3,2,1,0:T(1,128)} %param.21) | copy-start | bytes 3076
  80.6 111.9 %copy-start.2 = (s32[1,128]{1,0:T(1,128)S(1)}, s32[1,128]{1,0:T(1,128)}, u32[]{:S(2)}) copy-start(s32[1,128]{1,0:T(1,128)} %param.19) | copy-start | bytes 1540
  188.2 26.3 %all-to-all-start.2 = ((f32[32,2,1,8,256]{4,3,1,2,0:T(8,128)}), f32[32,2,1,8,256]{4,3,1,2,0:T(8,128)S(1)}, u32[]{:S(2)}, u32[]{:S(2)}) async-start(f32[32,2,1,8,256]{4,3,1,2,0:T(8,128)} %constant_dynamic-update-slice_fusion), calls=%async_computation.2 | async-start | bytes 1048576 | tf_op jit(solution)/shard_map/all_to_all | solution.py:81
  214.4 26.4 %all-to-all-start.3 = ((f32[2,32,8,256]{3,2,0,1:T(8,128)}), f32[2,32,8,256]{3,2,0,1:T(8,128)S(1)}, u32[]{:S(2)}, u32[]{:S(2)}) async-start(f32[2,32,8,256]{3,2,0,1:T(8,128)} %bitcast.64), calls=%async_computation.3 | async-start | bytes 1048576 | tf_op jit(solution)/shard_map/all_to_all | solution.py:86
  283.2 26.5 %all-to-all-start.5 = ((f32[2,1,256,256]{3,0,1,2:T(2,128)}), f32[2,1,256,256]{3,0,1,2:T(2,128)S(1)}, u32[]{:S(2)}, u32[]{:S(2)}) async-start(f32[2,1,256,256]{3,0,1,2:T(2,128)} %copy.98), calls=%async_computation.5 | async-start | bytes 1048576 | tf_op jit(solution)/shard_map/all_to_all | solution.py:74
  309.7 26.3 %all-to-all-start.4 = ((f32[2,1,256,256]{3,0,1,2:T(2,128)}), f32[2,1,256,256]{3,0,1,2:T(2,128)S(1)}, u32[]{:S(2)}, u32[]{:S(2)}) async-start(f32[2,1,256,256]{3,0,1,2:T(2,128)} %copy.95), calls=%async_computation.4 | async-start | bytes 1048576 | tf_op jit(solution)/shard_map/all_to_all | solution.py:73
  441.5 26.3 %all-to-all-start.7 = ((f32[2,32,8,256]{3,2,0,1:T(8,128)}), f32[2,32,8,256]{3,2,0,1:T(8,128)S(1)}, u32[]{:S(2)}, u32[]{:S(2)}) async-start(f32[2,32,8,256]{3,2,0,1:T(8,128)} %bitcast.142), calls=%async_computation.7 | async-start | bytes 1048576 | tf_op jit(solution)/shard_map/all_to_all | solution.py:86
  467.7 26.3 %all-to-all-start.6 = ((f32[32,2,1,8,256]{4,3,1,2,0:T(8,128)}), f32[32,2,1,8,256]{4,3,1,2,0:T(8,128)S(1)}, u32[]{:S(2)}, u32[]{:S(2)}) async-start(f32[32,2,1,8,256]{4,3,1,2,0:T(8,128)} %constant_dynamic-update-slice_fusion.32), calls=%async_computation.6 | async-start | bytes 1048576 | tf_op jit(solution)/shard_map/all_to_all | solution.py:81
  472.1 176.3 %all-reduce.3.cloned.1.call-start = ((), (), s32[]{:S(2)}) async-start(), calls=%async_computation.8 | async-start | bytes 131072 | tf_op jit(solution)/shard_map/psum | solution.py:138
Sparse Core Ops, SparseCore 0:
  501.9 146.4 all-reduce.2
